TPU v7x, 32 devices: a whole 2x2x4 slice. The times are simulated.
32 devices in a mesh: groups: 2 (over y), cells: 8 (over z, core), narrow: 2 (over x).
Axes of the slice: x: 2, y: 2, z: 4, core: 2. Of those that a mesh axis runs over, the one named last changes fastest.
Arguments:
- queries: bfloat16 [256, 1024], P(('groups', 'cells', 'narrow')), parts along dimension 0, may hold values from -6 to 6
- probes: int32 [256, 8], P(('groups', 'cells', 'narrow')), parts along dimension 0, may hold values from 0 to 15, all different within a row; in each aligned block of 8 rows (0 to 7, 8 to 15, ...) at most 8 rows name the same one
- cell_slot: int32 [16], replicated, may hold values from 0 to 15, each once
- centroids: float32 [16, 1024], P('cells'), may hold values from -4 to 4
- rotations: bfloat16 [16, 1024, 1024], P('cells', None, 'narrow'), may hold values from -0.1875 to 0.1875
- codebooks: bfloat16 [16, 64, 16, 256], P('cells', 'narrow'), may hold values from -6 to 6
Outputs:
- tables: bfloat16 [16, 2, 128, 64, 256], P(('groups', 'cells'), 'narrow'), parts along dimension 0
There are 2 independent parts, one for each index of `groups`. A program takes and returns all parts, laid end to end along the dimension named above; an argument that names none is the same for every part. Nothing has to cross between parts.
Inputs may be any that keep to these rules, and one draw needn't show every extreme that they name: `probes`: each query names 8 different cells. Among the queries of one aligned block of 8 no cell is named more than 8 times, a bound that some block reaches. `cell_slot`: each storage position is held by exactly one cell.
All inputs are finite; a program needn't handle non-finite values.
Results may differ from a plain program's by a relative error of at most 0.0043.
Values may be sent and summed in bfloat16 or wider, within the bound.
A program may use at most 64 MiB of HBM per device.

v0:
```python
import jax
import jax.numpy as jnp
from jax import lax
from jax.sharding import PartitionSpec as P


def subspace_tables(rotated, books):
    width = books.shape[2]
    parts = rotated.reshape(rotated.shape[:-1] + (books.shape[1], width))
    cross = jnp.einsum("...lsmt,lmtk->...lsmk", parts, books, preferred_element_type=jnp.float32)
    wide = parts.astype(jnp.float32)
    own = jnp.sum(wide * wide, axis=-1)
    word = jnp.sum(jnp.square(books.astype(jnp.float32)), axis=2)
    return (own[..., None] - 2.0 * cross + word[:, None, :, :]) / width


def per_device(queries, probes, cell_slot, centroids, rotations, codebooks):
    q_dev, probe_count = probes.shape
    cells_all = cell_slot.shape[0]
    cell_dev = centroids.shape[0]
    depth = queries.shape[1]
    most = min(q_dev, max(2, 2 * q_dev * probe_count // cells_all))
    owners = lax.axis_size("cells")
    span = jnp.arange(cells_all, dtype=jnp.int32)
    owner_hot = (cell_slot[:, None] == span[None, :]).astype(jnp.int32)
    probe_hot = (probes.reshape(-1)[:, None] == span[None, :]).astype(jnp.int32)
    position_hot = jnp.dot(probe_hot, owner_hot)
    rank = jnp.sum((jnp.cumsum(position_hot, axis=0) - position_hot) * position_hot, axis=1)
    position = jnp.dot(position_hot, span)
    slot = position * most + rank
    slot_span = jnp.arange(cells_all * most, dtype=jnp.int32)
    assign = jnp.sum(
        (slot[:, None] == slot_span[None, :])
        .astype(jnp.int32)
        .reshape(q_dev, probe_count, cells_all * most),
        axis=1,
    )
    assign_bf = assign.astype(jnp.bfloat16)
    send = jnp.einsum("qs,qd->sd", assign_bf, queries, preferred_element_type=jnp.float32).astype(
        jnp.bfloat16
    )
    valid = jnp.sum(assign, axis=0).astype(jnp.bfloat16)
    rows, marks = (
        lax.all_to_all(
            send.reshape(owners, cell_dev * most, depth),
            "cells",
            split_axis=0,
            concat_axis=0,
            tiled=True,
        ),
        lax.all_to_all(
            valid.reshape(owners, cell_dev * most), "cells", split_axis=0, concat_axis=0, tiled=True
        ),
    )
    rows = rows.reshape(owners, cell_dev, most, depth)
    marks = marks.reshape(owners, cell_dev, most)
    residual = (rows.astype(jnp.float32) - centroids[None, :, None, :]).astype(jnp.bfloat16)
    rotated = jnp.einsum(
        "nilsd,lde->nilse",
        lax.all_gather(residual[None], "narrow", axis=0, tiled=True),
        rotations,
        preferred_element_type=jnp.float32,
    ).astype(jnp.bfloat16)
    gathered = subspace_tables(rotated, codebooks).astype(jnp.bfloat16)
    mine = lax.all_to_all(gathered, "narrow", split_axis=0, concat_axis=4, tiled=True)[0]
    table = mine * marks[..., None, None]
    return table.reshape((1, 1, owners * cell_dev * most) + table.shape[-2:])


def solution(mesh):
    return jax.shard_map(
        per_device,
        mesh=mesh,
        in_specs=(
            P(("groups", "cells", "narrow"), None),
            P(("groups", "cells", "narrow"), None),
            P(),
            P("cells", None),
            P("cells", None, "narrow"),
            P("cells", "narrow", None, None),
        ),
        out_specs=P(("groups", "cells"), "narrow", None, None, None),
        check_vma=False,
    )
```

profile of v0, /device:TPU:0, one launch (start us, length us, event | category | flops | bytes accessed | tf_op | source)
XLA Modules:
  0.0 105.5 jit_solution(4467672718814948187)
XLA Ops:
  0.0 0.0 copy-start
  0.0 0.9 eq.44
  0.9 0.9 fusion.16
  1.8 0.1 copy.34
  1.9 0.1 reduce_window_sum.11
  2.0 0.1 copy.35
  2.1 0.1 fusion.13
  2.2 0.1 eq.51
  2.3 0.1 convert_reduce_fusion
  2.4 1.7 %convolution_convert_fusion = bf16[128,1024]{1,0:T(8,128)(2,1)} fusion(bf16[8,1024]{1,0:T(8,128)(2,1)} %param.6, s32[8,128]{1,0:T(8,128)S(1)} %get-tuple-element.6), kind=kOutput, calls=%fused_computation.10 | convolution fusion | flops 2229248 | bytes 282624 | tf_op jit(solution)/shard_map/qs,qd->sd/dot_general | solution.py:39
  4.1 6.3 %all-to-all-start = ((bf16[8,16,1024]{2,1,0:T(8,128)(2,1)}), bf16[8,16,1024]{2,1,0:T(8,128)(2,1)S(1)}, u32[]{:S(2)}, u32[]{:S(2)}) async-start(bf16[8,16,1024]{2,1,0:T(8,128)(2,1)} %bitcast.1), calls=%async_computation | async-start | bytes 524288 | tf_op jit(solution)/shard_map/all_to_all | solution.py:44
  10.4 0.7 convert_element_type.78
  11.1 1.3 %multiply_reduce_fusion.1 = f32[2,32,256]{2,1,0:T(8,128)S(1)} fusion(bf16[2,32,16,256]{3,2,1,0:T(8,128)(2,1)} %param.11), kind=kLoop, calls=%fused_computation.15 | loop fusion | flops 770048 | bytes 589824 | tf_op jit(solution)/shard_map/reduce_sum | solution.py:13
  12.4 7.8 %all-to-all-done = bf16[8,16,1024]{2,1,0:T(8,128)(2,1)S(1)} async-done(((bf16[8,16,1024]{2,1,0:T(8,128)(2,1)}), bf16[8,16,1024]{2,1,0:T(8,128)(2,1)S(1)}, u32[]{:S(2)}, u32[]{:S(2)}) %all-to-all-start) | async-done | bytes 262176 | tf_op jit(solution)/shard_map/all_to_all | solution.py:44
  20.2 3.3 %all-to-all-start.2 = ((bf16[8,1,16]{2,1,0:T(2,128)(2,1)}), bf16[8,1,16]{2,1,0:T(2,128)(2,1)S(1)}, u32[]{:S(2)}, u32[]{:S(2)}) async-start(bf16[8,1,16]{2,1,0:T(2,128)(2,1)} %convert_element_type.78), calls=%async_computation.2 | async-start | bytes 8192 | tf_op jit(solution)/shard_map/all_to_all | solution.py:51
  23.5 0.7 fusion.15
  24.3 9.3 %all_gather.3 = bf16[2,8,2,8,1024]{4,3,1,0,2:T(8,128)(2,1)S(1)} all-gather(bf16[1,8,2,8,1024]{4,3,1,0,2:T(8,128)(2,1)S(1)} %fusion.15), channel_id=1, replica_groups=mesh['groups'=2,'cells'=8,'narrow'=2] {'narrow'}, dimensions={0}, use_global_device_ids=true | all-gather | bytes 786432 | tf_op jit(solution)/shard_map/all_gather | solution.py:60
  33.6 0.0 copy-done
  33.6 0.0 copy-start.1
  33.6 0.4 fusion.9
  34.1 2.7 %reshape.72 = bf16[2,8,2,8,32,16]{5,4,3,2,1,0:T(8,128)(2,1)} reshape(bf16[2,8,2,8,512]{4,3,2,1,0:T(8,128)(2,1)S(1)} %copy.37) | data formatting | bytes 524288 | tf_op jit(solution)/shard_map/reshape | solution.py:9
  36.7 2.7 %multiply_reduce_fusion = f32[2,8,2,8,32]{4,3,2,1,0:T(8,128)S(1)} fusion(bf16[2,8,2,8,32,16]{5,4,3,2,1,0:T(8,128)(2,1)} %reshape.72), kind=kLoop, calls=%fused_computation.4 | loop fusion | flops 385024 | bytes 294912 | tf_op jit(solution)/shard_map/reduce_sum | solution.py:12
  39.5 0.3 copy.38
  39.8 0.0 copy-done.1
  39.8 3.3 %fusion.2 = bf16[2,8,2,8,32,256]{5,3,1,0,4,2:T(8,128)(2,1)S(1)} fusion(f32[2,32,256]{2,1,0:T(8,128)S(1)} %multiply_reduce_fusion.1, f32[2,8,2,8,32]{3,1,0,4,2:T(8,128)S(1)} %copy.38, bf16[2,8,2,8,32,16]{5,4,3,2,1,0:T(8,128)(2,1)} %reshape.72, bf16[2,32,16,256]{3,2,1,0:T(8,128)(2,1)S(1)} %copy-done.1), kind=kOutput, calls=%fused_computation.3 | convolution fusion | flops 77594624 | bytes 5079040 | tf_op jit(solution)/shard_map/...lsmt,lmtk->...lsmk/dot_general | solution.py:10
  43.1 2.3 %copy.40 = bf16[2,8,2,8,32,256]{5,3,1,4,2,0:T(8,128)(2,1)} copy(bf16[2,8,2,8,32,256]{5,3,1,0,4,2:T(8,128)(2,1)S(1)} %fusion.2) | data formatting | bytes 8388608 | tf_op jit(solution)/shard_map/convert_element_type | solution.py:64
  45.4 0.0 all-to-all-done.2
  45.5 5.6 %all-to-all-start.1 = ((bf16[2,8,2,8,32,256]{5,3,1,4,2,0:T(8,128)(2,1)}), bf16[2,8,2,8,32,256]{5,3,1,4,2,0:T(8,128)(2,1)}, u32[]{:S(2)}, u32[]{:S(2)}) async-start(bf16[2,8,2,8,32,256]{5,3,1,4,2,0:T(8,128)(2,1)} %copy.40), calls=%async_computation.1 | async-start | bytes 8388608 | tf_op jit(solution)/shard_map/all_to_all | solution.py:65
  51.1 0.1 mul.45
  51.2 47.4 %all-to-all-done.1 = bf16[2,8,2,8,32,256]{5,3,1,4,2,0:T(8,128)(2,1)} async-done(((bf16[2,8,2,8,32,256]{5,3,1,4,2,0:T(8,128)(2,1)}), bf16[2,8,2,8,32,256]{5,3,1,4,2,0:T(8,128)(2,1)}, u32[]{:S(2)}, u32[]{:S(2)}) %all-to-all-start.1) | async-done | bytes 4194336 | tf_op jit(solution)/shard_map/all_to_all | solution.py:65
  98.6 4.6 %copy.41 = bf16[2,8,2,8,32,256]{5,4,0,3,2,1:T(8,128)(2,1)S(1)} copy(bf16[2,8,2,8,32,256]{5,3,1,4,2,0:T(8,128)(2,1)} %all-to-all-done.1) | data formatting | bytes 8388608 | tf_op jit(solution)/shard_map/all_to_all | solution.py:65
  103.1 2.4 %broadcast_multiply_fusion = bf16[1,1,128,64,256]{4,3,2,1,0:T(8,128)(2,1)} fusion(bf16[1,1,128,64,256]{4,3,2,1,0:T(8,128)(2,1)S(1)} %bitcast.45, bf16[128]{0:T(256)(128)(2,1)S(1)} %mul.45), kind=kLoop, calls=%fused_computation.8 | loop fusion | flops 2097152 | bytes 8388864 | tf_op jit(solution)/shard_map/mul | solution.py:66
  (4 shorter events, 0.1 us)
Async XLA Ops:
  0.0 33.6 %copy-start = (bf16[2,1024,512]{2,1,0:T(8,128)(2,1)S(1)}, bf16[2,1024,512]{2,1,0:T(8,128)(2,1)}, u32[]{:S(2)}) copy-start(bf16[2,1024,512]{2,1,0:T(8,128)(2,1)} %param.10) | copy-start | bytes 6291460
  4.1 16.1 %all-to-all-start = ((bf16[8,16,1024]{2,1,0:T(8,128)(2,1)}), bf16[8,16,1024]{2,1,0:T(8,128)(2,1)S(1)}, u32[]{:S(2)}, u32[]{:S(2)}) async-start(bf16[8,16,1024]{2,1,0:T(8,128)(2,1)} %bitcast.1), calls=%async_computation | async-start | bytes 524288 | tf_op jit(solution)/shard_map/all_to_all | solution.py:44
  20.2 25.3 %all-to-all-start.2 = ((bf16[8,1,16]{2,1,0:T(2,128)(2,1)}), bf16[8,1,16]{2,1,0:T(2,128)(2,1)S(1)}, u32[]{:S(2)}, u32[]{:S(2)}) async-start(bf16[8,1,16]{2,1,0:T(2,128)(2,1)} %convert_element_type.78), calls=%async_computation.2 | async-start | bytes 8192 | tf_op jit(solution)/shard_map/all_to_all | solution.py:51
  33.6 6.2 %copy-start.1 = (bf16[2,32,16,256]{3,2,1,0:T(8,128)(2,1)S(1)}, bf16[2,32,16,256]{3,2,1,0:T(8,128)(2,1)}, u32[]{:S(2)}) copy-start(bf16[2,32,16,256]{3,2,1,0:T(8,128)(2,1)} %param.11) | copy-start | bytes 1572868
  45.5 53.1 %all-to-all-start.1 = ((bf16[2,8,2,8,32,256]{5,3,1,4,2,0:T(8,128)(2,1)}), bf16[2,8,2,8,32,256]{5,3,1,4,2,0:T(8,128)(2,1)}, u32[]{:S(2)}, u32[]{:S(2)}) async-start(bf16[2,8,2,8,32,256]{5,3,1,4,2,0:T(8,128)(2,1)} %copy.40), calls=%async_computation.1 | async-start | bytes 8388608 | tf_op jit(solution)/shard_map/all_to_all | solution.py:65
where the time goes:
time: 106 us; the launch traced here: 105 us
  waiting for transfers between devices  55.2 us (52%)
  starting transfers between devices  15.3 us (14%)
  local copies, waits for them, and re-layouts  11.8 us (11%)
  blocking collectives  9.32 us (9%)
  other arithmetic  7.36 us (7%)
  matrix products  6.5 us (6%)
    all_to_all x1, waiting for transfers between devices, per_device(): lax.all_to_all(gathered, 'narrow', split_axis=0, concat_axis=4, tiled=True)  47.4 us
    all_gather x1, blocking collectives, per_device(): lax.all_gather(residual[None], 'narrow', axis=0, tiled=True)  9.32 us
    all_to_all x1, waiting for transfers between devices, per_device(): lax.all_to_all(send.reshape(owners, cell_dev * most, depth), 'cells', spl...  7.79 us
    all_to_all x1, starting transfers between devices, per_device(): lax.all_to_all(send.reshape(owners, cell_dev * most, depth), 'cells', spl...  6.33 us
    all_to_all x1, starting transfers between devices, per_device(): lax.all_to_all(gathered, 'narrow', split_axis=0, concat_axis=4, tiled=True)  5.62 us
    all_to_all x1, local copies, waits for them, and re-layouts, per_device(): lax.all_to_all(gathered, 'narrow', split_axis=0, concat_axis=4, tiled=True)  4.56 us
    all_to_all x1, starting transfers between devices, per_device(): lax.all_to_all(valid.reshape(owners, cell_dev * most), 'cells', split_axi...  3.33 us
    dot_general x1, matrix products, subspace_tables(): jnp.einsum('...lsmt,lmtk->...lsmk', parts, books, preferred_element_type=...  3.32 us
  transfers between devices with their start and end apart: 3, of which 2 were waited for; matrix products, arithmetic and copies ran while one was open for 14% of the time, Pallas kernels for 0%

commit v1 on v0

v1 whole, which is shorter than its diff:
```python
import functools

import jax
import jax.numpy as jnp
from jax import lax
from jax.experimental import pallas as pl
from jax.experimental.pallas import tpu as pltpu
from jax.sharding import PartitionSpec as P

MESH = pl.DeviceIdType.MESH
F32 = jnp.float32
BF16 = jnp.bfloat16
LANES = 128


def most_of(q_dev, probe_count, cells_all):
    return min(q_dev, max(2, 2 * q_dev * probe_count // cells_all))


def exchange_kernel(
    owners, most, slot_of, queries, probes, centroids, rotations, books,
    x_out, books_out, marks_out,
    blocks, turn, x_send, q_send_sem, q_recv_sem, b_sem, r_sem, local_sem,
):
    q_dev, depth = queries.shape
    probe_count = probes.shape[1]
    cell_dev, half_m = books.shape[:2]
    half = rotations.shape[2]
    cells_all = slot_of.shape[0]
    rows = owners * q_dev
    slots = owners * most
    g = lax.axis_index("groups")
    j = lax.axis_index("cells")
    n = lax.axis_index("narrow")
    other = 1 - n

    load = pltpu.make_async_copy(rotations, turn, local_sem.at[0])
    load.start()
    keep = pltpu.make_async_copy(
        books, books_out.at[:, pl.ds(n * half_m, half_m)], local_sem.at[1]
    )
    keep.start()

    peers = [(dj, dn) for dn in (1, 0) for dj in range(owners) if (dj, dn) != (0, 0)]

    def target(dj, dn):
        return (g, lax.rem(j + dj, owners), lax.rem(n + dn, 2))

    barrier = pltpu.get_barrier_semaphore()
    for dj, dn in peers:
        pl.semaphore_signal(barrier, inc=1, device_id=target(dj, dn), device_id_type=MESH)

    blocks[n, j, :, :depth] = queries[...]
    tail = jnp.concatenate(
        [probes[...].astype(F32), jnp.zeros((q_dev, LANES - probe_count), F32)], axis=1
    )
    blocks[n, j, :, depth:] = tail.astype(BF16)
    pl.semaphore_wait(barrier, len(peers))

    sends = []
    for k, (dj, dn) in enumerate(peers):
        copy = pltpu.make_async_remote_copy(
            src_ref=blocks.at[n, j],
            dst_ref=blocks.at[n, j],
            send_sem=q_send_sem.at[k],
            recv_sem=q_recv_sem.at[k],
            device_id=target(dj, dn),
            device_id_type=MESH,
        )
        copy.start()
        sends.append(copy)
    mine = pl.ds(n * half_m, half_m)
    books_copy = pltpu.make_async_remote_copy(
        src_ref=books,
        dst_ref=books_out.at[:, mine],
        send_sem=b_sem.at[0],
        recv_sem=b_sem.at[1],
        device_id=(g, j, other),
        device_id_type=MESH,
    )
    books_copy.start()

    def arrived(dn):
        for k, (dj, kn) in enumerate(peers):
            if kn == dn:
                source = blocks.at[lax.rem(n + 2 - dn, 2), lax.rem(j + owners - dj, owners)]
                pltpu.make_async_remote_copy(
                    src_ref=source,
                    dst_ref=source,
                    send_sem=q_send_sem.at[k],
                    recv_sem=q_recv_sem.at[k],
                    device_id=target(dj, dn),
                    device_id_type=MESH,
                ).wait_recv()

    row = lax.broadcasted_iota(jnp.int32, (rows, rows), 0)
    col = lax.broadcasted_iota(jnp.int32, (rows, rows), 1)
    earlier = ((row < col) & (row // q_dev == col // q_dev)).astype(F32).astype(BF16)
    slot_row = lax.broadcasted_iota(jnp.int32, (slots, rows), 0)
    slot_col = lax.broadcasted_iota(jnp.int32, (slots, rows), 1)
    same = (slot_row // most == slot_col // q_dev).astype(F32)
    place = (slot_row % most).astype(F32)

    def cell_at(position):
        cell = jnp.int32(0)
        for c in range(cells_all):
            cell = cell + jnp.where(slot_of[c] == position, c, 0)
        return cell

    cells = [cell_at(j * cell_dev + l).astype(F32) for l in range(cell_dev)]

    def column(which):
        wide = blocks[which].astype(F32).reshape(rows, depth + LANES)
        named = wide[:, depth:]
        lane = lax.broadcasted_iota(jnp.int32, (rows, LANES), 1) < probe_count
        out = []
        for l in range(cell_dev):
            hit = ((named == cells[l]) & lane).astype(F32).astype(BF16)
            hits = lax.dot_general(
                jnp.ones((8, LANES), BF16), hit, (((1,), (1,)), ((), ())),
                preferred_element_type=F32,
            )
            rank = jnp.dot(hits.astype(BF16), earlier, preferred_element_type=F32)
            pick = (place == rank[:1]).astype(F32) * hits[:1] * same
            residual = (wide[:, :depth] - centroids[l : l + 1]).astype(BF16)
            rotated = jnp.dot(residual, turn[l], preferred_element_type=F32).astype(BF16)
            x = jnp.dot(pick.astype(BF16), rotated, preferred_element_type=F32).astype(BF16)
            out.append((x, pick))
        return out

    here = pl.ds(pl.multiple_of(n * half, LANES), half)
    load.wait()
    arrived(1)
    for l, (x, _) in enumerate(column(other)):
        x_send[l] = x
    x_copy = pltpu.make_async_remote_copy(
        src_ref=x_send,
        dst_ref=x_out.at[:, :, here],
        send_sem=r_sem.at[0],
        recv_sem=r_sem.at[1],
        device_id=(g, j, other),
        device_id_type=MESH,
    )
    x_copy.start()
    arrived(0)
    for l, (x, pick) in enumerate(column(n)):
        x_out[l, :, here] = x
        marks_out[l] = jnp.broadcast_to(
            jnp.sum(pick, axis=1, keepdims=True), marks_out.shape[1:]
        )
    keep.wait()
    for copy in sends:
        copy.wait_send()
    x_copy.wait()
    books_copy.wait()


def table_kernel(x_ref, books_ref, marks_ref, out_ref):
    _, group, width, words = books_ref.shape
    slots, span = x_ref.shape[1:]
    blocks, _, most = out_ref.shape[:3]
    lane = lax.broadcasted_iota(jnp.int32, (group, span), 1)
    row = lax.broadcasted_iota(jnp.int32, (group, span), 0)
    mask = (lane // width == row).astype(F32)
    book = books_ref[0].reshape(group * width, words)
    wide = books_ref[0].astype(F32)
    word = jnp.sum(wide * wide, axis=1)
    x = x_ref[0].astype(F32)
    spread = x[:, None, :] * mask[None]
    own = jnp.sum(spread * spread, axis=2, keepdims=True)
    cross = jnp.dot(
        spread.astype(BF16).reshape(slots * group, span), book, preferred_element_type=F32
    ).reshape(slots, group, words)
    marks = marks_ref[0] * (1.0 / width)
    table = (own - 2.0 * cross + word[None]) * marks[:, None, :]
    out_ref[...] = table.astype(BF16).reshape(blocks, 1, most, group, words)


def two_narrow(queries, probes, cell_slot, centroids, rotations, codebooks):
    q_dev, probe_count = probes.shape
    cells_all = cell_slot.shape[0]
    cell_dev, half_m, width, words = codebooks.shape
    depth = queries.shape[1]
    half = rotations.shape[2]
    owners = lax.axis_size("cells")
    most = most_of(q_dev, probe_count, cells_all)
    slots = owners * most
    peers = 2 * owners - 1
    vmem = pl.BlockSpec(memory_space=pltpu.VMEM)
    anywhere = pl.BlockSpec(memory_space=pl.ANY)
    x, books, marks = pl.pallas_call(
        functools.partial(exchange_kernel, owners, most),
        name="exchange",
        out_shape=(
            jax.ShapeDtypeStruct((cell_dev, slots, depth), BF16),
            jax.ShapeDtypeStruct((cell_dev, 2 * half_m, width, words), BF16),
            jax.ShapeDtypeStruct((cell_dev, slots, words), F32),
        ),
        in_specs=[
            pl.BlockSpec(memory_space=pltpu.SMEM), vmem, vmem, vmem, anywhere, anywhere,
        ],
        out_specs=(vmem, anywhere, vmem),
        scratch_shapes=[
            pltpu.VMEM((2, owners, q_dev, depth + LANES), BF16),
            pltpu.VMEM(rotations.shape, BF16),
            pltpu.VMEM((cell_dev, slots, half), BF16),
            pltpu.SemaphoreType.DMA((peers,)),
            pltpu.SemaphoreType.DMA((peers,)),
            pltpu.SemaphoreType.DMA((2,)),
            pltpu.SemaphoreType.DMA((2,)),
            pltpu.SemaphoreType.DMA((2,)),
        ],
        compiler_params=pltpu.CompilerParams(
            collective_id=0, has_side_effects=True, vmem_limit_bytes=32 << 20
        ),
    )(cell_slot, queries, probes, centroids, rotations, codebooks)

    group = 16
    groups = 2 * half_m // group
    table = pl.pallas_call(
        table_kernel,
        name="tables",
        grid=(cell_dev, groups),
        out_shape=jax.ShapeDtypeStruct(
            (owners, cell_dev, most, 2 * half_m, words), BF16
        ),
        in_specs=[
            pl.BlockSpec((1, slots, group * width), lambda l, m: (l, 0, m)),
            pl.BlockSpec((1, group, width, words), lambda l, m: (l, m, 0, 0)),
            pl.BlockSpec((1, slots, words), lambda l, m: (l, 0, 0)),
        ],
        out_specs=pl.BlockSpec(
            (owners, 1, most, group, words), lambda l, m: (0, l, 0, m, 0)
        ),
        compiler_params=pltpu.CompilerParams(vmem_limit_bytes=32 << 20),
    )(x, books, marks)
    return table.reshape(1, 1, owners * cell_dev * most, 2 * half_m, words)


def subspace_tables(rotated, books):
    width = books.shape[2]
    parts = rotated.reshape(rotated.shape[:-1] + (books.shape[1], width))
    cross = jnp.einsum("...lsmt,lmtk->...lsmk", parts, books, preferred_element_type=F32)
    wide = parts.astype(F32)
    own = jnp.sum(wide * wide, axis=-1)
    word = jnp.sum(jnp.square(books.astype(F32)), axis=2)
    return (own[..., None] - 2.0 * cross + word[:, None, :, :]) / width


def any_narrow(queries, probes, cell_slot, centroids, rotations, codebooks):
    q_dev, probe_count = probes.shape
    cells_all = cell_slot.shape[0]
    cell_dev = centroids.shape[0]
    depth = queries.shape[1]
    most = most_of(q_dev, probe_count, cells_all)
    owners = lax.axis_size("cells")
    span = jnp.arange(cells_all, dtype=jnp.int32)
    owner_hot = (cell_slot[:, None] == span[None, :]).astype(jnp.int32)
    probe_hot = (probes.reshape(-1)[:, None] == span[None, :]).astype(jnp.int32)
    position_hot = jnp.dot(probe_hot, owner_hot)
    rank = jnp.sum((jnp.cumsum(position_hot, axis=0) - position_hot) * position_hot, axis=1)
    position = jnp.dot(position_hot, span)
    slot = position * most + rank
    slot_span = jnp.arange(cells_all * most, dtype=jnp.int32)
    assign = jnp.sum(
        (slot[:, None] == slot_span[None, :])
        .astype(jnp.int32)
        .reshape(q_dev, probe_count, cells_all * most),
        axis=1,
    )
    send = jnp.einsum(
        "qs,qd->sd", assign.astype(BF16), queries, preferred_element_type=F32
    ).astype(BF16)
    valid = jnp.sum(assign, axis=0).astype(BF16)
    rows = lax.all_to_all(
        send.reshape(owners, cell_dev * most, depth), "cells", split_axis=0, concat_axis=0, tiled=True
    ).reshape(owners, cell_dev, most, depth)
    marks = lax.all_to_all(
        valid.reshape(owners, cell_dev * most), "cells", split_axis=0, concat_axis=0, tiled=True
    ).reshape(owners, cell_dev, most)
    residual = (rows.astype(F32) - centroids[None, :, None, :]).astype(BF16)
    rotated = jnp.einsum(
        "nilsd,lde->nilse",
        lax.all_gather(residual[None], "narrow", axis=0, tiled=True),
        rotations,
        preferred_element_type=F32,
    ).astype(BF16)
    gathered = subspace_tables(rotated, codebooks).astype(BF16)
    mine = lax.all_to_all(gathered, "narrow", split_axis=0, concat_axis=4, tiled=True)[0]
    table = mine * marks[..., None, None]
    return table.reshape((1, 1, owners * cell_dev * most) + table.shape[-2:])


def solution(mesh):
    return jax.shard_map(
        two_narrow if mesh.shape["narrow"] == 2 else any_narrow,
        mesh=mesh,
        in_specs=(
            P(("groups", "cells", "narrow"), None),
            P(("groups", "cells", "narrow"), None),
            P(),
            P("cells", None),
            P("cells", None, "narrow"),
            P("cells", "narrow", None, None),
        ),
        out_specs=P(("groups", "cells"), "narrow", None, None, None),
        check_vma=False,
    )
```

time: 106 us -> 36.9 us (0.35)
  waiting for transfers between devices: 55.2 us -> 0 us
  Pallas kernels: 0 us -> 31.2 us
  starting transfers between devices: 15.3 us -> 0 us
  blocking collectives: 9.32 us -> 0 us
  other arithmetic: 7.36 us -> 0 us
  matrix products: 6.5 us -> 0 us
  local copies, waits for them, and re-layouts: 11.8 us -> 5.39 us
    all_to_all x3 -> x0, waiting for transfers between devices: 55.2 us -> none  [the longest x1 47.4 us: per_device(): lax.all_to_all(gathered, 'narrow', split_axis=0, concat_axis=4, tiled=True)]
    pallas_call x0 -> x2, Pallas kernels: none -> 31.2 us  [the longest x1 25.8 us: two_narrow(): pl.pallas_call(functools.partial(exchange_kernel, owners, most), name='ex...]
    all_to_all x3 -> x0, starting transfers between devices: 15.3 us -> none  [the longest x1 6.33 us: per_device(): lax.all_to_all(send.reshape(owners, cell_dev * most, depth), 'cells', spl...]
    all_gather x1 -> x0, blocking collectives: 9.32 us -> none  [per_device(): lax.all_gather(residual[None], 'narrow', axis=0, tiled=True)]
    dot_general x5 -> x0, matrix products: 6.5 us -> none  [the longest x1 3.32 us: subspace_tables(): jnp.einsum('...lsmt,lmtk->...lsmk', parts, books, preferred_element_type=...]
    unnamed x4 -> x12, local copies, waits for them, and re-layouts: 0.01 us -> 5.39 us
    all_to_all x1 -> x0, local copies, waits for them, and re-layouts: 4.56 us -> none  [per_device(): lax.all_to_all(gathered, 'narrow', split_axis=0, concat_axis=4, tiled=True)]
    reduce_sum x4 -> x0, other arithmetic: 4.13 us -> none  [the longest x1 2.75 us: subspace_tables(): own = jnp.sum(wide * wide, axis=-1)]
  transfers between devices with their start and end apart: 3 -> 0, of which waited for: 2 -> 0; matrix products, arithmetic and copies ran while one was open for 14% -> 0% of each run, Pallas kernels for 0% -> 0%
where the time goes in v1:
time: 36.9 us; the launch traced here: 36.6 us
  Pallas kernels  31.2 us (85%)
  local copies, waits for them, and re-layouts  5.39 us (15%)
    pallas_call x1, Pallas kernels, two_narrow(): pl.pallas_call(functools.partial(exchange_kernel, owners, most), name='ex...  25.8 us
    pallas_call x1, Pallas kernels, two_narrow(): pl.pallas_call(table_kernel, name='tables', grid=(cell_dev, groups), out_...  5.39 us
    unnamed x12, local copies, waits for them, and re-layouts  5.39 us

profile of v1, /device:TPU:0, one launch (start us, length us, event | category | flops | bytes accessed | tf_op | source)
XLA Modules:
  0.0 36.6 jit_solution(14757658630582503906)
XLA Ops:
  0.0 0.0 copy-start
  0.0 1.6 %copy-done = bf16[2,1024,512]{2,1,0:T(8,128)(2,1)S(1)} copy-done((bf16[2,1024,512]{2,1,0:T(8,128)(2,1)S(1)}, bf16[2,1024,512]{2,1,0:T(8,128)(2,1)}, u32[]{:S(2)}) %copy-start) | copy-done | bytes 2097176
  1.6 0.0 copy-start.1
  1.6 1.0 %copy-done.1 = bf16[2,32,16,256]{3,2,1,0:T(8,128)(2,1)S(1)} copy-done((bf16[2,32,16,256]{3,2,1,0:T(8,128)(2,1)S(1)}, bf16[2,32,16,256]{3,2,1,0:T(8,128)(2,1)}, u32[]{:S(2)}) %copy-start.1) | copy-done | bytes 524312
  2.6 0.0 copy-start.2
  2.6 0.7 %copy-done.2 = bf16[8,1024]{1,0:T(8,128)(2,1)S(1)} copy-done((bf16[8,1024]{1,0:T(8,128)(2,1)S(1)}, bf16[8,1024]{1,0:T(8,128)(2,1)}, u32[]{:S(2)}) %copy-start.2) | copy-done | bytes 16408
  3.4 0.0 copy-start.3
  3.4 0.7 %copy-done.3 = f32[2,1024]{1,0:T(2,128)S(1)} copy-done((f32[2,1024]{1,0:T(2,128)S(1)}, f32[2,1024]{1,0:T(2,128)}, u32[]{:S(2)}) %copy-start.3) | copy-done | bytes 8216
  4.0 0.0 copy-start.4
  4.1 0.7 %copy-done.4 = s32[8,8]{1,0:T(8,128)S(1)} copy-done((s32[8,8]{1,0:T(8,128)S(1)}, s32[8,8]{1,0:T(8,128)}, u32[]{:S(2)}) %copy-start.4) | copy-done | bytes 280
  4.7 0.0 copy-start.5
  4.7 0.7 %copy-done.5 = s32[16]{0:T(128)S(1)} copy-done((s32[16]{0:T(128)S(1)}, s32[16]{0:T(128)}, u32[]{:S(2)}) %copy-start.5) | copy-done | bytes 88
  5.4 25.8 %exchange.1 = (bf16[2,64,1024]{2,1,0:T(8,128)(2,1)S(1)}, bf16[2,64,16,256]{3,2,1,0:T(8,128)(2,1)S(1)}, f32[2,64,256]{2,1,0:T(8,128)S(1)}) custom-call(s32[16]{0:T(128)S(1)} %copy-done.5, bf16[8,1024]{1,0:T(8,128)(2,1)S(1)} %copy-done.2, s32[8,8]{1,0:T(8,128)S(1)} %copy-done.4, f32[2,1024]{1,0:T(2,128)S(1)} %copy-done.3, bf16[2,1024,512]{2,1,0:T(8,128)(2,1)S(1)} %copy-done, ...), custom_call_target="tpu_custom_call" | custom-call | tf_op jit(solution)/shard_map/exchange/pallas_call | solution.py:191
  31.2 5.4 %tables.1 = bf16[8,2,8,64,256]{4,3,2,1,0:T(8,128)(2,1)} custom-call(bf16[2,64,1024]{2,1,0:T(8,128)(2,1)S(1)} %get-tuple-element.8.x_ref, bf16[2,64,16,256]{3,2,1,0:T(8,128)(2,1)S(1)} %get-tuple-element.9.books_ref, f32[2,64,256]{2,1,0:T(8,128)S(1)} %get-tuple-element.10.marks_ref), custom_call_target="tpu_custom_call" | custom-call | tf_op jit(solution)/shard_map/tables/pallas_call | solution.py:220
Async XLA Ops:
  0.0 1.6 %copy-start = (bf16[2,1024,512]{2,1,0:T(8,128)(2,1)S(1)}, bf16[2,1024,512]{2,1,0:T(8,128)(2,1)}, u32[]{:S(2)}) copy-start(bf16[2,1024,512]{2,1,0:T(8,128)(2,1)} %rotations.1) | copy-start | bytes 6291460
  1.6 1.0 %copy-start.1 = (bf16[2,32,16,256]{3,2,1,0:T(8,128)(2,1)S(1)}, bf16[2,32,16,256]{3,2,1,0:T(8,128)(2,1)}, u32[]{:S(2)}) copy-start(bf16[2,32,16,256]{3,2,1,0:T(8,128)(2,1)} %books.1) | copy-start | bytes 1572868
  2.6 0.7 %copy-start.2 = (bf16[8,1024]{1,0:T(8,128)(2,1)S(1)}, bf16[8,1024]{1,0:T(8,128)(2,1)}, u32[]{:S(2)}) copy-start(bf16[8,1024]{1,0:T(8,128)(2,1)} %queries.1) | copy-start | bytes 49156
  3.4 0.7 %copy-start.3 = (f32[2,1024]{1,0:T(2,128)S(1)}, f32[2,1024]{1,0:T(2,128)}, u32[]{:S(2)}) copy-start(f32[2,1024]{1,0:T(2,128)} %centroids.1) | copy-start | bytes 24580
  4.0 0.7 %copy-start.4 = (s32[8,8]{1,0:T(8,128)S(1)}, s32[8,8]{1,0:T(8,128)}, u32[]{:S(2)}) copy-start(s32[8,8]{1,0:T(8,128)} %probes.1) | copy-start | bytes 772
  4.7 0.7 %copy-start.5 = (s32[16]{0:T(128)S(1)}, s32[16]{0:T(128)}, u32[]{:S(2)}) copy-start(s32[16]{0:T(128)} %slot_of.1) | copy-start | bytes 196

commit v2 on v1

--- a/solution.py
+++ b/solution.py
@@ -18,44 +18,58 @@
 
 
 def exchange_kernel(
-    owners, most, slot_of, queries, probes, centroids, rotations, books,
+    owners, most, slot_hbm, queries_hbm, probes_hbm, centroids_hbm, rotations, books,
     x_out, books_out, marks_out,
-    blocks, turn, x_send, q_send_sem, q_recv_sem, b_sem, r_sem, local_sem,
+    blocks, turn, x_send, slot_of, probes, centroids,
+    q_send_sem, q_recv_sem, b_send_sem, b_recv_sem, y_send_sem, y_recv_sem, r_sem, local_sem,
 ):
-    q_dev, depth = queries.shape
+    q_dev, depth = queries_hbm.shape
     probe_count = probes.shape[1]
     cell_dev, half_m = books.shape[:2]
     half = rotations.shape[2]
     cells_all = slot_of.shape[0]
     rows = owners * q_dev
     slots = owners * most
+    pieces = b_send_sem.shape[0]
+    step = half_m // pieces
     g = lax.axis_index("groups")
     j = lax.axis_index("cells")
     n = lax.axis_index("narrow")
     other = 1 - n
 
-    load = pltpu.make_async_copy(rotations, turn, local_sem.at[0])
-    load.start()
-    keep = pltpu.make_async_copy(
-        books, books_out.at[:, pl.ds(n * half_m, half_m)], local_sem.at[1]
-    )
-    keep.start()
-
     peers = [(dj, dn) for dn in (1, 0) for dj in range(owners) if (dj, dn) != (0, 0)]
 
     def target(dj, dn):
         return (g, lax.rem(j + dj, owners), lax.rem(n + dn, 2))
 
+    across = (1 - g, j, n)
     barrier = pltpu.get_barrier_semaphore()
     for dj, dn in peers:
         pl.semaphore_signal(barrier, inc=1, device_id=target(dj, dn), device_id_type=MESH)
-
-    blocks[n, j, :, :depth] = queries[...]
+    pl.semaphore_signal(barrier, inc=1, device_id=across, device_id_type=MESH)
+
+    loads = [
+        pltpu.make_async_copy(src, dst, local_sem.at[i])
+        for i, (src, dst) in enumerate(
+            [
+                (queries_hbm, blocks.at[n, j, :, pl.ds(0, depth)]),
+                (probes_hbm, probes),
+                (slot_hbm, slot_of),
+                (centroids_hbm, centroids),
+                (rotations, turn),
+                (books, books_out.at[:, pl.ds(n * half_m, half_m)]),
+            ]
+        )
+    ]
+    for load in loads:
+        load.start()
+    loads[1].wait()
     tail = jnp.concatenate(
         [probes[...].astype(F32), jnp.zeros((q_dev, LANES - probe_count), F32)], axis=1
     )
     blocks[n, j, :, depth:] = tail.astype(BF16)
-    pl.semaphore_wait(barrier, len(peers))
+    loads[0].wait()
+    pl.semaphore_wait(barrier, len(peers) + 1)
 
     sends = []
     for k, (dj, dn) in enumerate(peers):
@@ -69,16 +83,33 @@
         )
         copy.start()
         sends.append(copy)
-    mine = pl.ds(n * half_m, half_m)
-    books_copy = pltpu.make_async_remote_copy(
-        src_ref=books,
-        dst_ref=books_out.at[:, mine],
-        send_sem=b_sem.at[0],
-        recv_sem=b_sem.at[1],
-        device_id=(g, j, other),
-        device_id_type=MESH,
-    )
-    books_copy.start()
+    firsts = []
+    for p in range(pieces):
+        copy = pltpu.make_async_remote_copy(
+            src_ref=books.at[g, pl.ds(p * step, step)],
+            dst_ref=books_out.at[g, pl.ds(n * half_m + p * step, step)],
+            send_sem=b_send_sem.at[p],
+            recv_sem=b_recv_sem.at[p],
+            device_id=(g, j, other),
+            device_id_type=MESH,
+        )
+        copy.start()
+        firsts.append(copy)
+    relays = []
+
+    def relay(p):
+        firsts[p].wait_recv()
+        piece = books_out.at[g, pl.ds(other * half_m + p * step, step)]
+        copy = pltpu.make_async_remote_copy(
+            src_ref=piece,
+            dst_ref=piece,
+            send_sem=y_send_sem.at[p],
+            recv_sem=y_recv_sem.at[p],
+            device_id=across,
+            device_id_type=MESH,
+        )
+        copy.start()
+        relays.append(copy)
 
     def arrived(dn):
         for k, (dj, kn) in enumerate(peers):
@@ -107,6 +138,8 @@
             cell = cell + jnp.where(slot_of[c] == position, c, 0)
         return cell
 
+    loads[2].wait()
+    loads[3].wait()
     cells = [cell_at(j * cell_dev + l).astype(F32) for l in range(cell_dev)]
 
     def column(which):
@@ -129,7 +162,9 @@
         return out
 
     here = pl.ds(pl.multiple_of(n * half, LANES), half)
-    load.wait()
+    for p in range(pieces // 2):
+        relay(p)
+    loads[4].wait()
     arrived(1)
     for l, (x, _) in enumerate(column(other)):
         x_send[l] = x
@@ -142,37 +177,72 @@
         device_id_type=MESH,
     )
     x_copy.start()
+    for p in range(pieces // 2, pieces):
+        relay(p)
     arrived(0)
     for l, (x, pick) in enumerate(column(n)):
         x_out[l, :, here] = x
         marks_out[l] = jnp.broadcast_to(
             jnp.sum(pick, axis=1, keepdims=True), marks_out.shape[1:]
         )
-    keep.wait()
-    for copy in sends:
+    loads[5].wait()
+    for copy in sends + firsts:
         copy.wait_send()
     x_copy.wait()
-    books_copy.wait()
+    for copy in relays:
+        copy.wait()
+
+
+def split3(value):
+    high = value.astype(BF16)
+    rest = value - high.astype(F32)
+    middle = rest.astype(BF16)
+    low = (rest - middle.astype(F32)).astype(BF16)
+    return high, middle, low
 
 
 def table_kernel(x_ref, books_ref, marks_ref, out_ref):
     _, group, width, words = books_ref.shape
     slots, span = x_ref.shape[1:]
     blocks, _, most = out_ref.shape[:3]
-    lane = lax.broadcasted_iota(jnp.int32, (group, span), 1)
-    row = lax.broadcasted_iota(jnp.int32, (group, span), 0)
-    mask = (lane // width == row).astype(F32)
-    book = books_ref[0].reshape(group * width, words)
+    scale = 1.0 / width
+    extra = LANES
+    third = 3 * group
+    lane = lax.broadcasted_iota(jnp.int32, (group, span + extra), 1)
+    row = lax.broadcasted_iota(jnp.int32, (group, span + extra), 0)
+    mask = (jnp.where(lane < span, lane // width, lane % group) == row).astype(F32)
+
     wide = books_ref[0].astype(F32)
-    word = jnp.sum(wide * wide, axis=1)
+    word = jnp.sum(wide * wide, axis=1) * scale
+    book = jnp.concatenate(
+        [
+            books_ref[0].reshape(group * width, words),
+            *split3(word),
+            jnp.ones((third, words), BF16),
+            jnp.zeros((extra - 2 * third, words), BF16),
+        ],
+        axis=0,
+    )
+
     x = x_ref[0].astype(F32)
-    spread = x[:, None, :] * mask[None]
-    own = jnp.sum(spread * spread, axis=2, keepdims=True)
-    cross = jnp.dot(
-        spread.astype(BF16).reshape(slots * group, span), book, preferred_element_type=F32
-    ).reshape(slots, group, words)
-    marks = marks_ref[0] * (1.0 / width)
-    table = (own - 2.0 * cross + word[None]) * marks[:, None, :]
+    square = x * x
+    high = square.astype(BF16)
+    low = (square - high.astype(F32)).astype(BF16)
+    at = lax.broadcasted_iota(jnp.int32, (span, extra), 0) // width
+    to = lax.broadcasted_iota(jnp.int32, (span, extra), 1)
+    gather = ((to % group == at) & (to >= third) & (to < 2 * third)).astype(F32)
+    gather = gather.astype(BF16)
+    own = scale * (
+        jnp.dot(high, gather, preferred_element_type=F32)
+        + jnp.dot(low, gather, preferred_element_type=F32)
+    )
+    tops = [part.astype(F32) for part in split3(own)]
+    spot = lax.broadcasted_iota(jnp.int32, (slots, extra), 1)
+    part = jnp.where(spot < third + group, tops[0], jnp.where(spot < third + 2 * group, tops[1], tops[2]))
+    part = jnp.where(spot < third, marks_ref[0], part)
+    left = jnp.concatenate([x * (-2.0 * scale), part], axis=1)
+    spread = (left[:, None, :] * mask[None]).astype(BF16).reshape(slots * group, span + extra)
+    table = jnp.dot(spread, book, preferred_element_type=F32)
     out_ref[...] = table.astype(BF16).reshape(blocks, 1, most, group, words)
 
 
@@ -187,31 +257,35 @@
     slots = owners * most
     peers = 2 * owners - 1
     vmem = pl.BlockSpec(memory_space=pltpu.VMEM)
-    anywhere = pl.BlockSpec(memory_space=pl.ANY)
+    pieces = 4
     x, books, marks = pl.pallas_call(
         functools.partial(exchange_kernel, owners, most),
         name="exchange",
         out_shape=(
             jax.ShapeDtypeStruct((cell_dev, slots, depth), BF16),
             jax.ShapeDtypeStruct((cell_dev, 2 * half_m, width, words), BF16),
-            jax.ShapeDtypeStruct((cell_dev, slots, words), F32),
-        ),
-        in_specs=[
-            pl.BlockSpec(memory_space=pltpu.SMEM), vmem, vmem, vmem, anywhere, anywhere,
-        ],
-        out_specs=(vmem, anywhere, vmem),
+            jax.ShapeDtypeStruct((cell_dev, slots, LANES), F32),
+        ),
+        in_specs=[pl.BlockSpec(memory_space=pltpu.HBM)] * 6,
+        out_specs=(vmem, pl.BlockSpec(memory_space=pl.ANY), vmem),
         scratch_shapes=[
             pltpu.VMEM((2, owners, q_dev, depth + LANES), BF16),
             pltpu.VMEM(rotations.shape, BF16),
             pltpu.VMEM((cell_dev, slots, half), BF16),
+            pltpu.SMEM(cell_slot.shape, jnp.int32),
+            pltpu.VMEM(probes.shape, jnp.int32),
+            pltpu.VMEM(centroids.shape, F32),
             pltpu.SemaphoreType.DMA((peers,)),
             pltpu.SemaphoreType.DMA((peers,)),
+            pltpu.SemaphoreType.DMA((pieces,)),
+            pltpu.SemaphoreType.DMA((pieces,)),
+            pltpu.SemaphoreType.DMA((pieces,)),
+            pltpu.SemaphoreType.DMA((pieces,)),
             pltpu.SemaphoreType.DMA((2,)),
-            pltpu.SemaphoreType.DMA((2,)),
-            pltpu.SemaphoreType.DMA((2,)),
+            pltpu.SemaphoreType.DMA((6,)),
         ],
         compiler_params=pltpu.CompilerParams(
-            collective_id=0, has_side_effects=True, vmem_limit_bytes=32 << 20
+            collective_id=0, has_side_effects=True, vmem_limit_bytes=64 << 20
         ),
     )(cell_slot, queries, probes, centroids, rotations, codebooks)
 
@@ -227,7 +301,7 @@
         in_specs=[
             pl.BlockSpec((1, slots, group * width), lambda l, m: (l, 0, m)),
             pl.BlockSpec((1, group, width, words), lambda l, m: (l, m, 0, 0)),
-            pl.BlockSpec((1, slots, words), lambda l, m: (l, 0, 0)),
+            pl.BlockSpec((1, slots, LANES), lambda l, m: (l, 0, 0)),
         ],
         out_specs=pl.BlockSpec(
             (owners, 1, most, group, words), lambda l, m: (0, l, 0, m, 0)
@@ -293,7 +367,7 @@
 
 def solution(mesh):
     return jax.shard_map(
-        two_narrow if mesh.shape["narrow"] == 2 else any_narrow,
+        two_narrow if mesh.shape["narrow"] == mesh.shape["groups"] == 2 else any_narrow,
         mesh=mesh,
         in_specs=(
             P(("groups", "cells", "narrow"), None),

time: 36.9 us -> 31.2 us (0.85)
  Pallas kernels: 31.2 us -> 27.9 us
  local copies, waits for them, and re-layouts: 5.39 us -> 3.01 us
    pallas_call x1, Pallas kernels: 25.8 us -> 21.8 us  [two_narrow(): pl.pallas_call(functools.partial(exchange_kernel, owners, most), name='ex...]
    unnamed x12 -> x6, local copies, waits for them, and re-layouts: 5.39 us -> 3.01 us
    pallas_call x1, Pallas kernels: 5.39 us -> 6.15 us  [two_narrow(): pl.pallas_call(table_kernel, name='tables', grid=(cell_dev, groups), out_...]
where the time goes in v2:
time: 31.2 us; the launch traced here: 30.9 us
  Pallas kernels  27.9 us (89%)
  local copies, waits for them, and re-layouts  3.01 us (10%)
    pallas_call x1, Pallas kernels, two_narrow(): pl.pallas_call(functools.partial(exchange_kernel, owners, most), name='ex...  21.8 us
    pallas_call x1, Pallas kernels, two_narrow(): pl.pallas_call(table_kernel, name='tables', grid=(cell_dev, groups), out_...  6.15 us
    unnamed x6, local copies, waits for them, and re-layouts  3.01 us

profile of v2, /device:TPU:0, one launch (start us, length us, event | category | flops | bytes accessed | tf_op | source)
XLA Modules:
  0.0 30.9 jit_solution(6499073052823972735)
XLA Ops:
  0.0 21.8 %exchange.1 = (bf16[2,64,1024]{2,1,0:T(8,128)(2,1)}, bf16[2,64,16,256]{3,2,1,0:T(8,128)(2,1)}, f32[2,64,128]{2,1,0:T(8,128)}) custom-call(s32[16]{0:T(128)} %slot_hbm.1, bf16[8,1024]{1,0:T(8,128)(2,1)} %queries_hbm.1, s32[8,8]{1,0:T(8,128)} %probes_hbm.1, f32[2,1024]{1,0:T(2,128)} %centroids_hbm.1, bf16[2,1024,512]{2,1,0:T(8,128)(2,1)} %rotations.1, ...), custom_call_target="tpu_custom_call" | custom-call | tf_op jit(solution)/shard_map/exchange/pallas_call | solution.py:261
  21.8 0.0 copy-start
  21.8 1.2 %copy-done = bf16[2,64,16,256]{3,2,1,0:T(8,128)(2,1)S(1)} copy-done((bf16[2,64,16,256]{3,2,1,0:T(8,128)(2,1)S(1)}, bf16[2,64,16,256]{3,2,1,0:T(8,128)(2,1)}, u32[]{:S(2)}) %copy-start) | copy-done | bytes 1048600
  23.0 0.0 copy-start.1
  23.0 0.9 %copy-done.1 = bf16[2,64,1024]{2,1,0:T(8,128)(2,1)S(1)} copy-done((bf16[2,64,1024]{2,1,0:T(8,128)(2,1)S(1)}, bf16[2,64,1024]{2,1,0:T(8,128)(2,1)}, u32[]{:S(2)}) %copy-start.1) | copy-done | bytes 262168
  23.9 0.0 copy-start.2
  23.9 0.8 %copy-done.2 = f32[2,64,128]{2,1,0:T(8,128)S(1)} copy-done((f32[2,64,128]{2,1,0:T(8,128)S(1)}, f32[2,64,128]{2,1,0:T(8,128)}, u32[]{:S(2)}) %copy-start.2) | copy-done | bytes 65560
  24.8 6.2 %tables.1 = bf16[8,2,8,64,256]{4,3,2,1,0:T(8,128)(2,1)} custom-call(bf16[2,64,1024]{2,1,0:T(8,128)(2,1)S(1)} %copy-done.1, bf16[2,64,16,256]{3,2,1,0:T(8,128)(2,1)S(1)} %copy-done, f32[2,64,128]{2,1,0:T(8,128)S(1)} %copy-done.2), custom_call_target="tpu_custom_call" | custom-call | tf_op jit(solution)/shard_map/tables/pallas_call | solution.py:294
Async XLA Ops:
  21.8 1.2 %copy-start = (bf16[2,64,16,256]{3,2,1,0:T(8,128)(2,1)S(1)}, bf16[2,64,16,256]{3,2,1,0:T(8,128)(2,1)}, u32[]{:S(2)}) copy-start(bf16[2,64,16,256]{3,2,1,0:T(8,128)(2,1)} %get-tuple-element.9.books_ref) | copy-start | bytes 3145732
  23.0 0.9 %copy-start.1 = (bf16[2,64,1024]{2,1,0:T(8,128)(2,1)S(1)}, bf16[2,64,1024]{2,1,0:T(8,128)(2,1)}, u32[]{:S(2)}) copy-start(bf16[2,64,1024]{2,1,0:T(8,128)(2,1)} %get-tuple-element.8.x_ref) | copy-start | bytes 786436
  23.9 0.8 %copy-start.2 = (f32[2,64,128]{2,1,0:T(8,128)S(1)}, f32[2,64,128]{2,1,0:T(8,128)}, u32[]{:S(2)}) copy-start(f32[2,64,128]{2,1,0:T(8,128)} %get-tuple-element.10.marks_ref) | copy-start | bytes 196612

commit v3 on v2

--- a/solution.py
+++ b/solution.py
@@ -11,6 +11,7 @@
 F32 = jnp.float32
 BF16 = jnp.bfloat16
 LANES = 128
+TABLE_STEPS = 2
 
 
 def most_of(q_dev, probe_count, cells_all):
@@ -57,7 +58,6 @@
                 (slot_hbm, slot_of),
                 (centroids_hbm, centroids),
                 (rotations, turn),
-                (books, books_out.at[:, pl.ds(n * half_m, half_m)]),
             ]
         )
     ]
@@ -87,7 +87,7 @@
     for p in range(pieces):
         copy = pltpu.make_async_remote_copy(
             src_ref=books.at[g, pl.ds(p * step, step)],
-            dst_ref=books_out.at[g, pl.ds(n * half_m + p * step, step)],
+            dst_ref=books_out.at[g, pl.ds(p * step, step)],
             send_sem=b_send_sem.at[p],
             recv_sem=b_recv_sem.at[p],
             device_id=(g, j, other),
@@ -99,7 +99,7 @@
 
     def relay(p):
         firsts[p].wait_recv()
-        piece = books_out.at[g, pl.ds(other * half_m + p * step, step)]
+        piece = books_out.at[g, pl.ds(p * step, step)]
         copy = pltpu.make_async_remote_copy(
             src_ref=piece,
             dst_ref=piece,
@@ -185,7 +185,6 @@
         marks_out[l] = jnp.broadcast_to(
             jnp.sum(pick, axis=1, keepdims=True), marks_out.shape[1:]
         )
-    loads[5].wait()
     for copy in sends + firsts:
         copy.wait_send()
     x_copy.wait()
@@ -201,49 +200,60 @@
     return high, middle, low
 
 
-def table_kernel(x_ref, books_ref, marks_ref, out_ref):
-    _, group, width, words = books_ref.shape
-    slots, span = x_ref.shape[1:]
+def table_kernel(x_ref, own_ref, far_ref, marks_ref, out_ref):
+    _, half_m, width, words = own_ref.shape
+    slots = x_ref.shape[1]
     blocks, _, most = out_ref.shape[:3]
+    group = 16
+    span = group * width
     scale = 1.0 / width
     extra = LANES
     third = 3 * group
+    n = lax.axis_index("narrow")
+
     lane = lax.broadcasted_iota(jnp.int32, (group, span + extra), 1)
     row = lax.broadcasted_iota(jnp.int32, (group, span + extra), 0)
     mask = (jnp.where(lane < span, lane // width, lane % group) == row).astype(F32)
-
-    wide = books_ref[0].astype(F32)
-    word = jnp.sum(wide * wide, axis=1) * scale
-    book = jnp.concatenate(
-        [
-            books_ref[0].reshape(group * width, words),
-            *split3(word),
-            jnp.ones((third, words), BF16),
-            jnp.zeros((extra - 2 * third, words), BF16),
-        ],
-        axis=0,
-    )
-
-    x = x_ref[0].astype(F32)
-    square = x * x
-    high = square.astype(BF16)
-    low = (square - high.astype(F32)).astype(BF16)
     at = lax.broadcasted_iota(jnp.int32, (span, extra), 0) // width
     to = lax.broadcasted_iota(jnp.int32, (span, extra), 1)
     gather = ((to % group == at) & (to >= third) & (to < 2 * third)).astype(F32)
     gather = gather.astype(BF16)
-    own = scale * (
-        jnp.dot(high, gather, preferred_element_type=F32)
-        + jnp.dot(low, gather, preferred_element_type=F32)
-    )
-    tops = [part.astype(F32) for part in split3(own)]
     spot = lax.broadcasted_iota(jnp.int32, (slots, extra), 1)
-    part = jnp.where(spot < third + group, tops[0], jnp.where(spot < third + 2 * group, tops[1], tops[2]))
-    part = jnp.where(spot < third, marks_ref[0], part)
-    left = jnp.concatenate([x * (-2.0 * scale), part], axis=1)
-    spread = (left[:, None, :] * mask[None]).astype(BF16).reshape(slots * group, span + extra)
-    table = jnp.dot(spread, book, preferred_element_type=F32)
-    out_ref[...] = table.astype(BF16).reshape(blocks, 1, most, group, words)
+    constant = [
+        jnp.ones((third, words), BF16),
+        jnp.zeros((extra - 2 * third, words), BF16),
+    ]
+
+    for books_ref, which in ((own_ref, n), (far_ref, 1 - n)):
+        for piece in range(half_m // group):
+            start = which * half_m + piece * group
+            books = books_ref[0, piece * group : (piece + 1) * group]
+            wide = books.astype(F32)
+            word = jnp.sum(wide * wide, axis=1) * scale
+            book = jnp.concatenate([books.reshape(span, words), *split3(word), *constant], axis=0)
+            x = x_ref[0, :, pl.ds(pl.multiple_of(start * width, span), span)].astype(F32)
+            square = x * x
+            high = square.astype(BF16)
+            low = (square - high.astype(F32)).astype(BF16)
+            own = scale * (
+                jnp.dot(high, gather, preferred_element_type=F32)
+                + jnp.dot(low, gather, preferred_element_type=F32)
+            )
+            tops = [part.astype(F32) for part in split3(own)]
+            part = jnp.where(
+                spot < third + group,
+                tops[0],
+                jnp.where(spot < third + 2 * group, tops[1], tops[2]),
+            )
+            part = jnp.where(spot < third, marks_ref[0], part)
+            left = jnp.concatenate([x * (-2.0 * scale), part], axis=1)
+            spread = (left[:, None, :] * mask[None]).astype(BF16)
+            table = jnp.dot(
+                spread.reshape(slots * group, span + extra), book, preferred_element_type=F32
+            )
+            out_ref[:, :, :, pl.ds(pl.multiple_of(start, group), group), :] = table.astype(
+                BF16
+            ).reshape(blocks, 1, most, group, words)
 
 
 def two_narrow(queries, probes, cell_slot, centroids, rotations, codebooks):
@@ -263,7 +273,7 @@
         name="exchange",
         out_shape=(
             jax.ShapeDtypeStruct((cell_dev, slots, depth), BF16),
-            jax.ShapeDtypeStruct((cell_dev, 2 * half_m, width, words), BF16),
+            jax.ShapeDtypeStruct(codebooks.shape, BF16),
             jax.ShapeDtypeStruct((cell_dev, slots, LANES), F32),
         ),
         in_specs=[pl.BlockSpec(memory_space=pltpu.HBM)] * 6,
@@ -282,32 +292,30 @@
             pltpu.SemaphoreType.DMA((pieces,)),
             pltpu.SemaphoreType.DMA((pieces,)),
             pltpu.SemaphoreType.DMA((2,)),
-            pltpu.SemaphoreType.DMA((6,)),
+            pltpu.SemaphoreType.DMA((5,)),
         ],
         compiler_params=pltpu.CompilerParams(
             collective_id=0, has_side_effects=True, vmem_limit_bytes=64 << 20
         ),
     )(cell_slot, queries, probes, centroids, rotations, codebooks)
 
-    group = 16
-    groups = 2 * half_m // group
+    part = max(owners // TABLE_STEPS, 1)
     table = pl.pallas_call(
         table_kernel,
         name="tables",
-        grid=(cell_dev, groups),
-        out_shape=jax.ShapeDtypeStruct(
-            (owners, cell_dev, most, 2 * half_m, words), BF16
-        ),
+        grid=(cell_dev, owners // part),
+        out_shape=jax.ShapeDtypeStruct((owners, cell_dev, most, 2 * half_m, words), BF16),
         in_specs=[
-            pl.BlockSpec((1, slots, group * width), lambda l, m: (l, 0, m)),
-            pl.BlockSpec((1, group, width, words), lambda l, m: (l, m, 0, 0)),
-            pl.BlockSpec((1, slots, LANES), lambda l, m: (l, 0, 0)),
+            pl.BlockSpec((1, part * most, depth), lambda l, i: (l, i, 0)),
+            pl.BlockSpec((1, half_m, width, words), lambda l, i: (l, 0, 0, 0)),
+            pl.BlockSpec((1, half_m, width, words), lambda l, i: (l, 0, 0, 0)),
+            pl.BlockSpec((1, part * most, LANES), lambda l, i: (l, i, 0)),
         ],
         out_specs=pl.BlockSpec(
-            (owners, 1, most, group, words), lambda l, m: (0, l, 0, m, 0)
+            (part, 1, most, 2 * half_m, words), lambda l, i: (i, l, 0, 0, 0)
         ),
-        compiler_params=pltpu.CompilerParams(vmem_limit_bytes=32 << 20),
-    )(x, books, marks)
+        compiler_params=pltpu.CompilerParams(vmem_limit_bytes=64 << 20),
+    )(x, codebooks, books, marks)
     return table.reshape(1, 1, owners * cell_dev * most, 2 * half_m, words)
 
 

time: 31.2 us -> 29.1 us (0.933)
  local copies, waits for them, and re-layouts: 3.01 us -> 0 us
  Pallas kernels: 27.9 us -> 28.8 us
    unnamed x6 -> x0, local copies, waits for them, and re-layouts: 3.01 us -> none
    pallas_call x1, Pallas kernels: 6.15 us -> 7.1 us  [two_narrow(): pl.pallas_call(table_kernel, name='tables', grid=(cell_dev, owners // par...]
where the time goes in v3:
time: 29.1 us; the launch traced here: 28.9 us
  Pallas kernels  28.8 us (99%)
    pallas_call x1, Pallas kernels, two_narrow(): pl.pallas_call(functools.partial(exchange_kernel, owners, most), name='ex...  21.7 us
    pallas_call x1, Pallas kernels, two_narrow(): pl.pallas_call(table_kernel, name='tables', grid=(cell_dev, owners // par...  7.1 us

profile of v3, /device:TPU:0, one launch (start us, length us, event | category | flops | bytes accessed | tf_op | source)
XLA Modules:
  0.0 28.9 jit_solution(15524454832152239286)
XLA Ops:
  0.0 21.7 %exchange.1 = (bf16[2,64,1024]{2,1,0:T(8,128)(2,1)}, bf16[2,32,16,256]{3,2,1,0:T(8,128)(2,1)}, f32[2,64,128]{2,1,0:T(8,128)}) custom-call(s32[16]{0:T(128)} %slot_hbm.1, bf16[8,1024]{1,0:T(8,128)(2,1)} %queries_hbm.1, s32[8,8]{1,0:T(8,128)} %probes_hbm.1, f32[2,1024]{1,0:T(2,128)} %centroids_hbm.1, bf16[2,1024,512]{2,1,0:T(8,128)(2,1)} %rotations.1, ...), custom_call_target="tpu_custom_call" | custom-call | tf_op jit(solution)/shard_map/exchange/pallas_call | solution.py:271
  21.8 7.1 %tables.1 = bf16[8,2,8,64,256]{4,3,2,1,0:T(8,128)(2,1)} custom-call(bf16[2,64,1024]{2,1,0:T(8,128)(2,1)} %get-tuple-element.8.x_ref, bf16[2,32,16,256]{3,2,1,0:T(8,128)(2,1)} %own_ref.1, bf16[2,32,16,256]{3,2,1,0:T(8,128)(2,1)} %get-tuple-element.9.far_ref, f32[2,64,128]{2,1,0:T(8,128)} %get-tuple-element.10.marks_ref), custom_call_target="tpu_custom_call" | custom-call | tf_op jit(solution)/shard_map/tables/pallas_call | solution.py:303

commit v4 on v3

--- a/solution.py
+++ b/solution.py
@@ -11,7 +11,7 @@
 F32 = jnp.float32
 BF16 = jnp.bfloat16
 LANES = 128
-TABLE_STEPS = 2
+TABLE_STEPS = 1
 
 
 def most_of(q_dev, probe_count, cells_all):
@@ -22,7 +22,7 @@
     owners, most, slot_hbm, queries_hbm, probes_hbm, centroids_hbm, rotations, books,
     x_out, books_out, marks_out,
     blocks, turn, x_send, slot_of, probes, centroids,
-    q_send_sem, q_recv_sem, b_send_sem, b_recv_sem, y_send_sem, y_recv_sem, r_sem, local_sem,
+    q_send_sem, q_recv_sem, b_send_sem, b_recv_sem, y_send_sem, y_recv_sem, x_send_sem, x_recv_sem, local_sem,
 ):
     q_dev, depth = queries_hbm.shape
     probe_count = probes.shape[1]
@@ -38,16 +38,22 @@
     n = lax.axis_index("narrow")
     other = 1 - n
 
-    peers = [(dj, dn) for dn in (1, 0) for dj in range(owners) if (dj, dn) != (0, 0)]
-
-    def target(dj, dn):
-        return (g, lax.rem(j + dj, owners), lax.rem(n + dn, 2))
+    hops = range(1, owners // 2)
+    beside = j + 1 - 2 * lax.rem(j, 2)
+    facing = (g, j, other)
+    paired = (g, beside, n)
+
+    def ahead(d):
+        return (g, lax.rem(j + 2 * d, owners), n)
+
+    def behind(cell, d):
+        return lax.rem(cell + owners - 2 * d, owners)
 
     across = (1 - g, j, n)
     barrier = pltpu.get_barrier_semaphore()
-    for dj, dn in peers:
-        pl.semaphore_signal(barrier, inc=1, device_id=target(dj, dn), device_id_type=MESH)
-    pl.semaphore_signal(barrier, inc=1, device_id=across, device_id_type=MESH)
+    partners = [facing, paired, across] + [ahead(d) for d in hops]
+    for partner in partners:
+        pl.semaphore_signal(barrier, inc=1, device_id=partner, device_id_type=MESH)
 
     loads = [
         pltpu.make_async_copy(src, dst, local_sem.at[i])
@@ -69,20 +75,38 @@
     )
     blocks[n, j, :, depth:] = tail.astype(BF16)
     loads[0].wait()
-    pl.semaphore_wait(barrier, len(peers) + 1)
-
-    sends = []
-    for k, (dj, dn) in enumerate(peers):
-        copy = pltpu.make_async_remote_copy(
-            src_ref=blocks.at[n, j],
-            dst_ref=blocks.at[n, j],
+    pl.semaphore_wait(barrier, len(partners))
+
+    def block_copy(k, column_at, cell, device):
+        return pltpu.make_async_remote_copy(
+            src_ref=blocks.at[column_at, cell],
+            dst_ref=blocks.at[column_at, cell],
             send_sem=q_send_sem.at[k],
             recv_sem=q_recv_sem.at[k],
-            device_id=target(dj, dn),
+            device_id=device,
             device_id_type=MESH,
         )
+
+    sends = []
+
+    def send(k, column_at, cell, device):
+        copy = block_copy(k, column_at, cell, device)
         copy.start()
         sends.append(copy)
+
+    count = 2 * len(hops) + 1
+
+    def from_behind(c, d):
+        return 1 + c * count + d - 1
+
+    def from_paired(c, d):
+        return 1 + c * count + len(hops) + d
+
+    columns = (n, other)
+    send(0, n, j, facing)
+    for d in hops:
+        send(from_behind(0, d), n, j, ahead(d))
+    send(from_paired(0, 0), n, j, paired)
     firsts = []
     for p in range(pieces):
         copy = pltpu.make_async_remote_copy(
@@ -111,18 +135,21 @@
         copy.start()
         relays.append(copy)
 
-    def arrived(dn):
-        for k, (dj, kn) in enumerate(peers):
-            if kn == dn:
-                source = blocks.at[lax.rem(n + 2 - dn, 2), lax.rem(j + owners - dj, owners)]
-                pltpu.make_async_remote_copy(
-                    src_ref=source,
-                    dst_ref=source,
-                    send_sem=q_send_sem.at[k],
-                    recv_sem=q_recv_sem.at[k],
-                    device_id=target(dj, dn),
-                    device_id_type=MESH,
-                ).wait_recv()
+    block_copy(0, other, j, facing).wait_recv()
+    for d in hops:
+        send(from_behind(1, d), other, j, ahead(d))
+    send(from_paired(1, 0), other, j, paired)
+
+    def pass_on(c):
+        for d in hops:
+            block_copy(from_behind(c, d), columns[c], behind(j, d), paired).wait_recv()
+            send(from_paired(c, d), columns[c], behind(j, d), paired)
+
+    def arrived(c):
+        for d in range(owners // 2):
+            block_copy(
+                from_paired(c, d), columns[c], behind(beside, d), paired
+            ).wait_recv()
 
     row = lax.broadcasted_iota(jnp.int32, (rows, rows), 0)
     col = lax.broadcasted_iota(jnp.int32, (rows, rows), 1)
@@ -146,7 +173,6 @@
         wide = blocks[which].astype(F32).reshape(rows, depth + LANES)
         named = wide[:, depth:]
         lane = lax.broadcasted_iota(jnp.int32, (rows, LANES), 1) < probe_count
-        out = []
         for l in range(cell_dev):
             hit = ((named == cells[l]) & lane).astype(F32).astype(BF16)
             hits = lax.dot_general(
@@ -158,26 +184,28 @@
             residual = (wide[:, :depth] - centroids[l : l + 1]).astype(BF16)
             rotated = jnp.dot(residual, turn[l], preferred_element_type=F32).astype(BF16)
             x = jnp.dot(pick.astype(BF16), rotated, preferred_element_type=F32).astype(BF16)
-            out.append((x, pick))
-        return out
+            yield x, pick
 
     here = pl.ds(pl.multiple_of(n * half, LANES), half)
-    for p in range(pieces // 2):
-        relay(p)
+    relay(0)
+    pass_on(1)
+    pass_on(0)
     loads[4].wait()
     arrived(1)
+    x_copies = []
     for l, (x, _) in enumerate(column(other)):
         x_send[l] = x
-    x_copy = pltpu.make_async_remote_copy(
-        src_ref=x_send,
-        dst_ref=x_out.at[:, :, here],
-        send_sem=r_sem.at[0],
-        recv_sem=r_sem.at[1],
-        device_id=(g, j, other),
-        device_id_type=MESH,
-    )
-    x_copy.start()
-    for p in range(pieces // 2, pieces):
+        copy = pltpu.make_async_remote_copy(
+            src_ref=x_send.at[l],
+            dst_ref=x_out.at[l, :, here],
+            send_sem=x_send_sem.at[l],
+            recv_sem=x_recv_sem.at[l],
+            device_id=facing,
+            device_id_type=MESH,
+        )
+        copy.start()
+        x_copies.append(copy)
+    for p in range(1, pieces):
         relay(p)
     arrived(0)
     for l, (x, pick) in enumerate(column(n)):
@@ -187,8 +215,7 @@
         )
     for copy in sends + firsts:
         copy.wait_send()
-    x_copy.wait()
-    for copy in relays:
+    for copy in x_copies + relays:
         copy.wait()
 
 
@@ -291,7 +318,8 @@
             pltpu.SemaphoreType.DMA((pieces,)),
             pltpu.SemaphoreType.DMA((pieces,)),
             pltpu.SemaphoreType.DMA((pieces,)),
-            pltpu.SemaphoreType.DMA((2,)),
+            pltpu.SemaphoreType.DMA((cell_dev,)),
+            pltpu.SemaphoreType.DMA((cell_dev,)),
             pltpu.SemaphoreType.DMA((5,)),
         ],
         compiler_params=pltpu.CompilerParams(
@@ -375,7 +403,7 @@
 
 def solution(mesh):
     return jax.shard_map(
-        two_narrow if mesh.shape["narrow"] == mesh.shape["groups"] == 2 else any_narrow,
+        two_narrow if mesh.shape["narrow"] == mesh.shape["groups"] == 2 and mesh.shape["cells"] % 2 == 0 else any_narrow,
         mesh=mesh,
         in_specs=(
             P(("groups", "cells", "narrow"), None),

time: 29.1 us -> 26.9 us (0.924)
  Pallas kernels: 28.8 us -> 26.7 us
    pallas_call x1, Pallas kernels: 21.7 us -> 20.6 us  [two_narrow(): pl.pallas_call(functools.partial(exchange_kernel, owners, most), name='ex...]
    pallas_call x1, Pallas kernels: 7.1 us -> 6.08 us  [two_narrow(): pl.pallas_call(table_kernel, name='tables', grid=(cell_dev, owners // par...]
where the time goes in v4:
time: 26.9 us; the launch traced here: 26.7 us
  Pallas kernels  26.7 us (99%)
    pallas_call x1, Pallas kernels, two_narrow(): pl.pallas_call(functools.partial(exchange_kernel, owners, most), name='ex...  20.6 us
    pallas_call x1, Pallas kernels, two_narrow(): pl.pallas_call(table_kernel, name='tables', grid=(cell_dev, owners // par...  6.08 us

profile of v4, /device:TPU:0, one launch (start us, length us, event | category | flops | bytes accessed | tf_op | source)
XLA Modules:
  0.0 26.7 jit_solution(15908706625837973515)
XLA Ops:
  0.0 20.6 %exchange.1 = (bf16[2,64,1024]{2,1,0:T(8,128)(2,1)}, bf16[2,32,16,256]{3,2,1,0:T(8,128)(2,1)}, f32[2,64,128]{2,1,0:T(8,128)}) custom-call(s32[16]{0:T(128)} %slot_hbm.1, bf16[8,1024]{1,0:T(8,128)(2,1)} %queries_hbm.1, s32[8,8]{1,0:T(8,128)} %probes_hbm.1, f32[2,1024]{1,0:T(2,128)} %centroids_hbm.1, bf16[2,1024,512]{2,1,0:T(8,128)(2,1)} %rotations.1, ...), custom_call_target="tpu_custom_call" | custom-call | tf_op jit(solution)/shard_map/exchange/pallas_call | solution.py:298
  20.6 6.1 %tables.1 = bf16[8,2,8,64,256]{4,3,2,1,0:T(8,128)(2,1)} custom-call(bf16[2,64,1024]{2,1,0:T(8,128)(2,1)} %get-tuple-element.8.x_ref, bf16[2,32,16,256]{3,2,1,0:T(8,128)(2,1)} %own_ref.1, bf16[2,32,16,256]{3,2,1,0:T(8,128)(2,1)} %get-tuple-element.9.far_ref, f32[2,64,128]{2,1,0:T(8,128)} %get-tuple-element.10.marks_ref), custom_call_target="tpu_custom_call" | custom-call | tf_op jit(solution)/shard_map/tables/pallas_call | solution.py:331

commit v5 on v4

--- a/solution.py
+++ b/solution.py
@@ -189,9 +189,13 @@
     here = pl.ds(pl.multiple_of(n * half, LANES), half)
     relay(0)
     pass_on(1)
+    relay(1)
     pass_on(0)
+    for p in range(2, pieces - 1):
+        relay(p)
     loads[4].wait()
     arrived(1)
+    relay(pieces - 1)
     x_copies = []
     for l, (x, _) in enumerate(column(other)):
         x_send[l] = x
@@ -205,8 +209,6 @@
         )
         copy.start()
         x_copies.append(copy)
-    for p in range(1, pieces):
-        relay(p)
     arrived(0)
     for l, (x, pick) in enumerate(column(n)):
         x_out[l, :, here] = x

time: 26.9 us -> 25.3 us (0.941)
  Pallas kernels: 26.7 us -> 25 us
    pallas_call x1, Pallas kernels: 20.6 us -> 18.9 us  [two_narrow(): pl.pallas_call(functools.partial(exchange_kernel, owners, most), name='ex...]
where the time goes in v5:
time: 25.3 us; the launch traced here: 25 us
  Pallas kernels  25 us (99%)
    pallas_call x1, Pallas kernels, two_narrow(): pl.pallas_call(functools.partial(exchange_kernel, owners, most), name='ex...  18.9 us
    pallas_call x1, Pallas kernels, two_narrow(): pl.pallas_call(table_kernel, name='tables', grid=(cell_dev, owners // par...  6.09 us

profile of v5, /device:TPU:0, one launch (start us, length us, event | category | flops | bytes accessed | tf_op | source)
XLA Modules:
  0.0 25.0 jit_solution(17316754601193769467)
XLA Ops:
  0.0 18.9 %exchange.1 = (bf16[2,64,1024]{2,1,0:T(8,128)(2,1)}, bf16[2,32,16,256]{3,2,1,0:T(8,128)(2,1)}, f32[2,64,128]{2,1,0:T(8,128)}) custom-call(s32[16]{0:T(128)} %slot_hbm.1, bf16[8,1024]{1,0:T(8,128)(2,1)} %queries_hbm.1, s32[8,8]{1,0:T(8,128)} %probes_hbm.1, f32[2,1024]{1,0:T(2,128)} %centroids_hbm.1, bf16[2,1024,512]{2,1,0:T(8,128)(2,1)} %rotations.1, ...), custom_call_target="tpu_custom_call" | custom-call | tf_op jit(solution)/shard_map/exchange/pallas_call | solution.py:300
  18.9 6.1 %tables.1 = bf16[8,2,8,64,256]{4,3,2,1,0:T(8,128)(2,1)} custom-call(bf16[2,64,1024]{2,1,0:T(8,128)(2,1)} %get-tuple-element.8.x_ref, bf16[2,32,16,256]{3,2,1,0:T(8,128)(2,1)} %own_ref.1, bf16[2,32,16,256]{3,2,1,0:T(8,128)(2,1)} %get-tuple-element.9.far_ref, f32[2,64,128]{2,1,0:T(8,128)} %get-tuple-element.10.marks_ref), custom_call_target="tpu_custom_call" | custom-call | tf_op jit(solution)/shard_map/tables/pallas_call | solution.py:333

commit v6 on v5

--- a/solution.py
+++ b/solution.py
@@ -221,14 +221,6 @@
         copy.wait()
 
 
-def split3(value):
-    high = value.astype(BF16)
-    rest = value - high.astype(F32)
-    middle = rest.astype(BF16)
-    low = (rest - middle.astype(F32)).astype(BF16)
-    return high, middle, low
-
-
 def table_kernel(x_ref, own_ref, far_ref, marks_ref, out_ref):
     _, half_m, width, words = own_ref.shape
     slots = x_ref.shape[1]
@@ -236,22 +228,12 @@
     group = 16
     span = group * width
     scale = 1.0 / width
-    extra = LANES
-    third = 3 * group
     n = lax.axis_index("narrow")
 
-    lane = lax.broadcasted_iota(jnp.int32, (group, span + extra), 1)
-    row = lax.broadcasted_iota(jnp.int32, (group, span + extra), 0)
-    mask = (jnp.where(lane < span, lane // width, lane % group) == row).astype(F32)
-    at = lax.broadcasted_iota(jnp.int32, (span, extra), 0) // width
-    to = lax.broadcasted_iota(jnp.int32, (span, extra), 1)
-    gather = ((to % group == at) & (to >= third) & (to < 2 * third)).astype(F32)
-    gather = gather.astype(BF16)
-    spot = lax.broadcasted_iota(jnp.int32, (slots, extra), 1)
-    constant = [
-        jnp.ones((third, words), BF16),
-        jnp.zeros((extra - 2 * third, words), BF16),
-    ]
+    lane = lax.broadcasted_iota(jnp.int32, (group, span), 1)
+    row = lax.broadcasted_iota(jnp.int32, (group, span), 0)
+    mask = (lane // width == row).astype(F32)
+    marks = jnp.concatenate([marks_ref[0]] * (words // LANES), axis=1)
 
     for books_ref, which in ((own_ref, n), (far_ref, 1 - n)):
         for piece in range(half_m // group):
@@ -259,27 +241,15 @@
             books = books_ref[0, piece * group : (piece + 1) * group]
             wide = books.astype(F32)
             word = jnp.sum(wide * wide, axis=1) * scale
-            book = jnp.concatenate([books.reshape(span, words), *split3(word), *constant], axis=0)
             x = x_ref[0, :, pl.ds(pl.multiple_of(start * width, span), span)].astype(F32)
-            square = x * x
-            high = square.astype(BF16)
-            low = (square - high.astype(F32)).astype(BF16)
-            own = scale * (
-                jnp.dot(high, gather, preferred_element_type=F32)
-                + jnp.dot(low, gather, preferred_element_type=F32)
-            )
-            tops = [part.astype(F32) for part in split3(own)]
-            part = jnp.where(
-                spot < third + group,
-                tops[0],
-                jnp.where(spot < third + 2 * group, tops[1], tops[2]),
-            )
-            part = jnp.where(spot < third, marks_ref[0], part)
-            left = jnp.concatenate([x * (-2.0 * scale), part], axis=1)
-            spread = (left[:, None, :] * mask[None]).astype(BF16)
+            spread = x[:, None, :] * mask[None]
+            own = jnp.sum(spread * spread, axis=2, keepdims=True) * scale
             table = jnp.dot(
-                spread.reshape(slots * group, span + extra), book, preferred_element_type=F32
-            )
+                (spread * (-2.0 * scale)).astype(BF16).reshape(slots * group, span),
+                books.reshape(span, words),
+                preferred_element_type=F32,
+            ).reshape(slots, group, words)
+            table = table + (own + word[None] * marks[:, None, :])
             out_ref[:, :, :, pl.ds(pl.multiple_of(start, group), group), :] = table.astype(
                 BF16
             ).reshape(blocks, 1, most, group, words)

time: 25.3 us -> 24.8 us (0.980)
  Pallas kernels: 25 us -> 24.6 us
    pallas_call x1, Pallas kernels: 6.09 us -> 5.68 us  [two_narrow(): pl.pallas_call(table_kernel, name='tables', grid=(cell_dev, owners // par...]
where the time goes in v6:
time: 24.8 us; the launch traced here: 24.6 us
  Pallas kernels  24.6 us (99%)
    pallas_call x1, Pallas kernels, two_narrow(): pl.pallas_call(functools.partial(exchange_kernel, owners, most), name='ex...  18.9 us
    pallas_call x1, Pallas kernels, two_narrow(): pl.pallas_call(table_kernel, name='tables', grid=(cell_dev, owners // par...  5.68 us

profile of v6, /device:TPU:0, one launch (start us, length us, event | category | flops | bytes accessed | tf_op | source)
XLA Modules:
  0.0 24.6 jit_solution(15139946895805272427)
XLA Ops:
  0.0 18.9 %exchange.1 = (bf16[2,64,1024]{2,1,0:T(8,128)(2,1)}, bf16[2,32,16,256]{3,2,1,0:T(8,128)(2,1)}, f32[2,64,128]{2,1,0:T(8,128)}) custom-call(s32[16]{0:T(128)} %slot_hbm.1, bf16[8,1024]{1,0:T(8,128)(2,1)} %queries_hbm.1, s32[8,8]{1,0:T(8,128)} %probes_hbm.1, f32[2,1024]{1,0:T(2,128)} %centroids_hbm.1, bf16[2,1024,512]{2,1,0:T(8,128)(2,1)} %rotations.1, ...), custom_call_target="tpu_custom_call" | custom-call | tf_op jit(solution)/shard_map/exchange/pallas_call | solution.py:270
  18.9 5.7 %tables.1 = bf16[8,2,8,64,256]{4,3,2,1,0:T(8,128)(2,1)} custom-call(bf16[2,64,1024]{2,1,0:T(8,128)(2,1)} %get-tuple-element.8.x_ref, bf16[2,32,16,256]{3,2,1,0:T(8,128)(2,1)} %own_ref.1, bf16[2,32,16,256]{3,2,1,0:T(8,128)(2,1)} %get-tuple-element.9.far_ref, f32[2,64,128]{2,1,0:T(8,128)} %get-tuple-element.10.marks_ref), custom_call_target="tpu_custom_call" | custom-call | tf_op jit(solution)/shard_map/tables/pallas_call | solution.py:303
